TPU v7x, 256 devices: a whole 4x4x8 slice. The times are simulated.
256 devices in a mesh: dp: 16 (over x_hi, y, core), tensor: 16 (over x_lo, z).
Axes of the slice: x: 4 (x_hi: 2, x_lo: 2; x = x_hi * 2 + x_lo), y: 4, z: 8, core: 2. Of those that a mesh axis runs over, the one named last changes fastest.
Arguments:
- tokens: bfloat16 [4096, 4096], P(('dp', 'tensor')), may hold values from -24 to 24
- gate_weight: bfloat16 [4096, 14336], P('dp', 'tensor'), may hold values from -0.09375 to 0.09375
- up_weight: bfloat16 [4096, 14336], P('dp', 'tensor'), may hold values from -0.09375 to 0.09375
- hidden_cotangent: bfloat16 [4096, 14336], P('dp', 'tensor'), may hold values from -1.5 to 1.5
Outputs:
- hidden: bfloat16 [4096, 14336], P('dp', 'tensor')
- grad_tokens: bfloat16 [4096, 4096], P(('dp', 'tensor'))
- grad_gate: bfloat16 [4096, 14336], P('dp', 'tensor')
- grad_up: bfloat16 [4096, 14336], P('dp', 'tensor')
All inputs are finite; a program needn't handle non-finite values.
Results may differ from a plain program's by a relative error of at most 0.023.
Values may be sent and summed in bfloat16 or wider, within the bound.
A program may use at most 64 MiB of HBM per device.

v0:
```python
import jax
import jax.numpy as jnp
from jax import lax
from jax.sharding import Mesh
from jax.sharding import PartitionSpec as P

SPLIT = ("xh", "c")
TENSOR = ("xl", "z")
DP = ("xh", "y", "c")
ROWS = P((*DP, *TENSOR), None)
BLOCK = P(DP, TENSOR)


def swiglu_parts(gate_pre, up_pre, cotangent):
    sigmoid_val = jax.nn.sigmoid(gate_pre)
    activation = gate_pre * sigmoid_val
    hidden = (activation * up_pre).astype(jnp.bfloat16)
    upstream = cotangent.astype(jnp.float32)
    slope = sigmoid_val * (1.0 + gate_pre * (1.0 - sigmoid_val))
    grad_gate_pre = (upstream * up_pre * slope).astype(jnp.bfloat16)
    grad_up_pre = (upstream * activation).astype(jnp.bfloat16)
    return (hidden, grad_gate_pre, grad_up_pre)


def body(tokens, gate_weight, up_weight, cotangent):
    rows, model = tokens.shape
    depth, width = gate_weight.shape
    nx, ny, nc = (lax.axis_size(a) for a in DP)
    nt = lax.axis_size(TENSOR)
    cut = tokens.reshape(rows, nx, ny, nc, depth).transpose(1, 3, 0, 2, 4)
    cut = cut.reshape(nx * nc, rows, ny * depth)
    cut = lax.all_to_all(cut, SPLIT, 0, 0, tiled=True)
    mine = lax.all_gather(cut, TENSOR, axis=1, tiled=True)
    mine = mine.reshape(nx * nc * nt * rows, ny * depth)
    weights = lax.all_gather(
        jnp.concatenate([gate_weight, up_weight], axis=1), "y", axis=0, tiled=True
    )
    part = jnp.dot(mine, weights, preferred_element_type=jnp.float32).astype(jnp.bfloat16)
    pre = lax.psum_scatter(part, SPLIT, scatter_dimension=0, tiled=True).astype(jnp.float32)
    hidden, grad_gate_pre, grad_up_pre = swiglu_parts(pre[:, :width], pre[:, width:], cotangent)
    grads = lax.all_gather(
        jnp.concatenate([grad_gate_pre, grad_up_pre], axis=1), SPLIT, axis=0, tiled=True
    )
    back = lax.dot_general(
        grads, weights, (((1,), (1,)), ((), ())), preferred_element_type=jnp.float32
    ).astype(jnp.bfloat16)
    nl, nz = (lax.axis_size(a) for a in TENSOR)
    back = back.reshape(nx * nc, nl, nz, rows, ny * depth).transpose(2, 1, 0, 3, 4)
    back = lax.psum_scatter(back, "z", scatter_dimension=0, tiled=True)[0]
    back = lax.psum_scatter(back, "xl", scatter_dimension=0, tiled=True)[0]
    back = lax.all_to_all(back, SPLIT, 0, 0, tiled=True)
    back = back.reshape(nx, nc, rows, ny, depth).transpose(2, 0, 3, 1, 4).reshape(rows, model)
    total = lax.dot_general(
        mine, grads, (((0,), (0,)), ((), ())), preferred_element_type=jnp.float32
    ).astype(jnp.bfloat16)
    total = lax.psum_scatter(total, "y", scatter_dimension=0, tiled=True)
    return (hidden, back, total[:, :width], total[:, width:])


def solution(mesh):
    torus = Mesh(mesh.devices.reshape(2, 4, 2, 2, 8), (*DP, *TENSOR))
    specs = (ROWS, BLOCK, BLOCK, BLOCK)
    outs = (BLOCK, ROWS, BLOCK, BLOCK)
    return jax.shard_map(body, mesh=torus, in_specs=specs, out_specs=outs, check_vma=False)
```

profile of v0, /device:TPU:1, one launch (start us, length us, event | category | flops | bytes accessed | tf_op | source)
XLA Modules:
  0.0 426.6 jit_solution(17104382645673480068)
XLA Ops:
  7.2 0.0 all-gather.6.cloned.1.call-start
  7.2 1.0 reshape.26
  8.2 0.1 copy.30
  8.3 0.1 reshape.27
  8.3 11.4 %all_to_all.10 = bf16[4,16,1024]{2,1,0:T(8,128)(2,1)} all-to-all(bf16[4,16,1024]{2,1,0:T(8,128)(2,1)S(1)} %reshape.27), channel_id=1, replica_groups=mesh['xh'=2,'y'=4,'c'=2,'xl'=2,'z'=8] {'xh','c'}, dimensions={0} | all-to-all | bytes 262144 | tf_op jit(solution)/shard_map/all_to_all | solution.py:32
  19.7 0.0 all-gather.6.cloned.1.call-update
  19.7 0.0 all-gather.4.cloned.1.call-start
  19.8 2.2 pad_maximum_fusion
  22.0 0.0 all-gather.4.cloned.1.call-update
  22.0 0.0 reduce-scatter.9.cloned.1.call-start
  22.0 60.2 %all-gather.6.cloned.1.call-done = bf16[4,256,1024]{2,1,0:T(8,128)(2,1)} async-done(((bf16[4,16,1024]{2,1,0:T(8,128)(2,1)}), bf16[4,256,1024]{2,1,0:T(8,128)(2,1)}) %all-gather.6.cloned.1.call-update) | async-done | bytes 2097168 | tf_op jit(solution)/shard_map/all_gather | solution.py:33
  82.2 55.2 %all-gather.4.cloned.1.call-done = bf16[1024,1792]{1,0:T(8,128)(2,1)} async-done(((bf16[256,1792]{1,0:T(8,128)(2,1)}), bf16[1024,1792]{1,0:T(8,128)(2,1)}) %all-gather.4.cloned.1.call-update) | async-done | bytes 3670032 | tf_op jit(solution)/shard_map/all_gather | solution.py:35
  137.4 8.6 %fusion = bf16[1024,1792]{0,1:T(8,128)(2,1)} fusion(bf16[1024,1792]{1,0:T(8,128)(2,1)} %all-gather.4.cloned.1.call-done, bf16[1024,1024]{1,0:T(8,128)(2,1)} %bitcast.41), kind=kOutput, calls=%fused_computation.2 | convolution fusion | flops 3759931392 | bytes 9437184 | tf_op jit(solution)/shard_map/dot_general | solution.py:38
  146.0 0.0 reduce-scatter.9.cloned.1.call-update
  146.0 0.0 all-gather.8.cloned.1.call-start
  146.0 0.9 copy-done
  147.0 0.2 copy.20
  147.2 52.5 %reduce-scatter.9.cloned.1.call-done = bf16[256,1792]{0,1:T(8,128)(2,1)} async-done(((bf16[1024,1792]{0,1:T(8,128)(2,1)}), bf16[256,1792]{0,1:T(8,128)(2,1)}) %reduce-scatter.9.cloned.1.call-update) | async-done | bytes 917520 | tf_op jit(solution)/shard_map/reduce_scatter | solution.py:39
  199.7 1.3 convert_element_type.32
  201.0 0.7 fusion.3
  201.7 1.0 pad_maximum_fusion.1
  202.6 0.0 all-gather.8.cloned.1.call-update
  202.7 0.0 all-reduce.5.cloned.1.call-start
  202.7 38.6 %all-gather.8.cloned.1.call-done = bf16[1024,1792]{0,1:T(8,128)(2,1)} async-done(((bf16[256,1792]{0,1:T(8,128)(2,1)}), bf16[1024,1792]{0,1:T(8,128)(2,1)}) %all-gather.8.cloned.1.call-update) | async-done | bytes 3670032 | tf_op jit(solution)/shard_map/all_gather | solution.py:41
  241.3 8.5 %convolution_convert_fusion.2 = bf16[1024,1024]{1,0:T(8,128)(2,1)} fusion(bf16[1024,1792]{0,1:T(8,128)(2,1)} %all-gather.8.cloned.1.call-done, bf16[1024,1792]{1,0:T(8,128)(2,1)} %all-gather.4.cloned.1.call-done), kind=kOutput, calls=%fused_computation.4 | convolution fusion | flops 3759144960 | bytes 9437184 | tf_op jit(solution)/shard_map/dot_general | solution.py:44
  249.8 0.0 all-reduce.5.cloned.1.call-update
  249.8 0.0 all-reduce.7.cloned.1.call-start
  249.9 0.6 dynamic-slice
  250.5 77.4 %all-reduce.5.cloned.1.call-done = bf16[8,2,4,16,1024]{4,3,0,1,2:T(8,128)(2,1)} async-done(((bf16[8,2,4,16,1024]{4,3,0,1,2:T(8,128)(2,1)}), bf16[8,2,4,16,1024]{4,3,0,1,2:T(8,128)(2,1)}) %all-reduce.5.cloned.1.call-update) | async-done | bytes 2097168
  327.9 2.3 dynamic-slice_bitcast_fusion
  330.2 0.0 all-reduce.7.cloned.1.call-update
  330.2 0.2 reduce-scatter.11.cloned.1.call-start
  330.5 7.6 %fusion.1 = bf16[1024,1792]{0,1:T(8,128)(2,1)} fusion(bf16[1024,1792]{0,1:T(8,128)(2,1)} %all-gather.8.cloned.1.call-done, bf16[1024,1024]{1,0:T(8,128)(2,1)S(1)} %bitcast.42), kind=kOutput, calls=%fused_computation.3 | convolution fusion | flops 3759931392 | bytes 9437184 | tf_op jit(solution)/shard_map/dot_general | solution.py:53
  338.0 0.0 reduce-scatter.11.cloned.1.call-update
  338.1 0.7 copy-done.2
  338.7 0.6 dynamic-slice.2
  339.3 28.0 %all-reduce.7.cloned.1.call-done = bf16[2,4,16,1024]{3,2,0,1:T(8,128)(2,1)} async-done(((bf16[2,4,16,1024]{3,2,0,1:T(8,128)(2,1)}), bf16[2,4,16,1024]{3,2,0,1:T(8,128)(2,1)}) %all-reduce.7.cloned.1.call-update) | async-done | bytes 262160
  367.3 2.2 dynamic-slice_bitcast_fusion.1
  369.6 5.1 %all-to-all-start.1 = ((bf16[4,16,1024]{2,1,0:T(8,128)(2,1)}), bf16[4,16,1024]{2,1,0:T(8,128)(2,1)S(1)}, u32[]{:S(2)}, u32[]{:S(2)}) async-start(bf16[4,16,1024]{2,1,0:T(8,128)(2,1)} %dynamic-slice_bitcast_fusion.1), calls=%async_computation.2 | async-start | bytes 262144 | tf_op jit(solution)/shard_map/all_to_all | solution.py:51
  374.6 1.0 copy.22
  375.6 4.1 all-to-all-done.1
  379.7 0.1 reshape.30
  379.8 0.1 copy.21
  380.0 0.7 reshape.31
  380.7 35.8 %reduce-scatter.11.cloned.1.call-done = bf16[256,1792]{0,1:T(8,128)(2,1)} async-done(((bf16[1024,1792]{0,1:T(8,128)(2,1)}), bf16[256,1792]{0,1:T(8,128)(2,1)}) %reduce-scatter.11.cloned.1.call-update) | async-done | bytes 917520 | tf_op jit(solution)/shard_map/reduce_scatter | solution.py:56
  416.5 1.2 fusion.6
  417.8 1.0 copy.23
  418.7 1.0 copy.24
  (6 shorter events, 0.0 us)
Async XLA Ops:
  7.2 75.0 %all-gather.6.cloned.1.call-start = ((), (), s32[]{:S(2)}) async-start(), calls=%async_computation.5 | async-start | bytes 2228224 | tf_op jit(solution)/shard_map/all_gather | solution.py:33
  19.7 117.6 %all-gather.4.cloned.1.call-start = ((), (), s32[]{:S(2)}) async-start(), calls=%async_computation.4 | async-start | bytes 4587520 | tf_op jit(solution)/shard_map/all_gather | solution.py:35
  22.0 177.7 %reduce-scatter.9.cloned.1.call-start = ((), (), s32[]{:S(2)}) async-start(), calls=%async_computation.6 | async-start | bytes 4587520 | tf_op jit(solution)/shard_map/reduce_scatter | solution.py:39
  146.0 1.0 copy-start
  146.0 95.3 %all-gather.8.cloned.1.call-start = ((), (), s32[]{:S(2)}) async-start(), calls=%async_computation.7 | async-start | bytes 4587520 | tf_op jit(solution)/shard_map/all_gather | solution.py:41
  202.7 47.2 %copy-start.3 = (u32[256]{0:T(256)S(1)}, u32[256]{0:T(256)}, u32[]{:S(2)}) copy-start(u32[256]{0:T(256)} %constant.5) | copy-start | bytes 3076
  202.7 127.8 %copy-start.1 = (bf16[4,256,1024]{2,1,0:T(8,128)(2,1)S(1)}, bf16[4,256,1024]{2,1,0:T(8,128)(2,1)}, u32[]{:S(2)}) copy-start(bf16[4,256,1024]{2,1,0:T(8,128)(2,1)} %all-gather.6.cloned.1.call-done) | copy-start | bytes 6291460
  202.7 125.2 %all-reduce.5.cloned.1.call-start = ((), (), s32[]{:S(2)}) async-start(), calls=%async_computation.9 | async-start | bytes 4194304
  249.8 117.5 %all-reduce.7.cloned.1.call-start = ((), (), s32[]{:S(2)}) async-start(), calls=%async_computation.10 | async-start | bytes 524288
  330.2 86.3 %reduce-scatter.11.cloned.1.call-start = ((), (), s32[]{:S(2)}) async-start(), calls=%async_computation.8 | async-start | bytes 4587520 | tf_op jit(solution)/shard_map/reduce_scatter | solution.py:56
  338.0 0.7 copy-start.2
  369.6 10.2 %all-to-all-start.1 = ((bf16[4,16,1024]{2,1,0:T(8,128)(2,1)}), bf16[4,16,1024]{2,1,0:T(8,128)(2,1)S(1)}, u32[]{:S(2)}, u32[]{:S(2)}) async-start(bf16[4,16,1024]{2,1,0:T(8,128)(2,1)} %dynamic-slice_bitcast_fusion.1), calls=%async_computation.2 | async-start | bytes 262144 | tf_op jit(solution)/shard_map/all_to_all | solution.py:51
Sparse Core Ops, SparseCore 0:
  19.9 62.2 all-gather.5
  84.0 53.2 all-gather.3
  146.1 53.5 reduce-scatter.8
  202.8 38.4 all-gather.7
  249.9 77.8 all-reduce.4
  331.0 36.2 all-reduce.6
  369.9 46.6 reduce-scatter.10
where the time goes:
time: 427 us
  waiting for transfers between devices  352 us (82%)
  matrix products  24.7 us (6%)
  between operations  14.2 us (3%)
  local copies, waits for them, and re-layouts  13.7 us (3%)
  blocking collectives  11.4 us (3%)
  starting transfers between devices  5.55 us (1%)
  other arithmetic  5.14 us (1%)
    unnamed x9, waiting for transfers between devices  106 us
    all_gather x1, waiting for transfers between devices, body(): mine = lax.all_gather(cut, TENSOR, axis=1, tiled=True)  60.2 us
    all_gather x1, waiting for transfers between devices, body(): lax.all_gather(jnp.concatenate([gate_weight, up_weight], axis=1), 'y', ax...  55.2 us
    reduce_scatter x1, waiting for transfers between devices, body(): lax.psum_scatter(part, SPLIT, scatter_dimension=0, tiled=True)  52.5 us
    all_gather x1, waiting for transfers between devices, body(): lax.all_gather(jnp.concatenate([grad_gate_pre, grad_up_pre], axis=1), SPL...  38.6 us
    reduce_scatter x1, waiting for transfers between devices, body(): total = lax.psum_scatter(total, 'y', scatter_dimension=0, tiled=True)  35.8 us
    all_to_all x1, blocking collectives, body(): cut = lax.all_to_all(cut, SPLIT, 0, 0, tiled=True)  11.4 us
    dot_general x1, matrix products, body(): jnp.dot(mine, weights, preferred_element_type=jnp.float32)  8.59 us
  transfers between devices with their start and end apart: 8, of which 8 were waited for; matrix products, arithmetic and copies ran while one was open for 4% of the time, Pallas kernels for 0%

commit v1 on v0

--- a/solution.py
+++ b/solution.py
@@ -30,7 +30,9 @@
     cut = tokens.reshape(rows, nx, ny, nc, depth).transpose(1, 3, 0, 2, 4)
     cut = cut.reshape(nx * nc, rows, ny * depth)
     cut = lax.all_to_all(cut, SPLIT, 0, 0, tiled=True)
-    mine = lax.all_gather(cut, TENSOR, axis=1, tiled=True)
+    mine = jnp.concatenate(
+        lax.all_to_all(jnp.stack([cut] * lax.axis_size(TENSOR)), TENSOR, 0, 0), axis=1
+    )
     mine = mine.reshape(nx * nc * nt * rows, ny * depth)
     weights = lax.all_gather(
         jnp.concatenate([gate_weight, up_weight], axis=1), "y", axis=0, tiled=True

time: 427 us -> 365 us (0.85)
  waiting for transfers between devices: 352 us -> 236 us
  blocking collectives: 11.4 us -> 65.5 us
    all_gather x1 -> x0, waiting for transfers between devices: 60.2 us -> none  [body(): mine = lax.all_gather(cut, TENSOR, axis=1, tiled=True)]
    all_gather x1, waiting for transfers between devices: 55.2 us -> 0.02 us  [body(): lax.all_gather(jnp.concatenate([gate_weight, up_weight], axis=1), 'y', ax...]
    all_to_all x0 -> x1, blocking collectives: none -> 54.8 us  [body(): lax.all_to_all(jnp.stack([cut] * lax.axis_size(TENSOR)), TENSOR, 0, 0)]
    unnamed x9 -> x8, waiting for transfers between devices: 106 us -> 106 us
  transfers between devices with their start and end apart: 8 -> 7, of which waited for: 8 -> 6; matrix products, arithmetic and copies ran while one was open for 4% -> 4% of each run, Pallas kernels for 0% -> 0%
where the time goes in v1:
time: 365 us
  waiting for transfers between devices  236 us (65%)
  blocking collectives  65.5 us (18%)
  matrix products  23.8 us (7%)
  between operations  14.2 us (4%)
  local copies, waits for them, and re-layouts  14.1 us (4%)
  starting transfers between devices  5.33 us (1%)
  other arithmetic  5.18 us (1%)
    unnamed x8, waiting for transfers between devices  106 us
    all_to_all x1, blocking collectives, body(): lax.all_to_all(jnp.stack([cut] * lax.axis_size(TENSOR)), TENSOR, 0, 0)  54.8 us
    reduce_scatter x1, waiting for transfers between devices, body(): lax.psum_scatter(part, SPLIT, scatter_dimension=0, tiled=True)  52.2 us
    all_gather x1, waiting for transfers between devices, body(): lax.all_gather(jnp.concatenate([grad_gate_pre, grad_up_pre], axis=1), SPL...  38.6 us
    reduce_scatter x1, waiting for transfers between devices, body(): total = lax.psum_scatter(total, 'y', scatter_dimension=0, tiled=True)  35.7 us
    all_to_all x1, blocking collectives, body(): cut = lax.all_to_all(cut, SPLIT, 0, 0, tiled=True)  10.7 us
    dot_general x1, matrix products, body(): lax.dot_general(grads, weights, (((1,), (1,)), ((), ())), preferred_eleme...  8.57 us
    dot_general x1, matrix products, body(): jnp.dot(mine, weights, preferred_element_type=jnp.float32)  7.71 us
  transfers between devices with their start and end apart: 7, of which 6 were waited for; matrix products, arithmetic and copies ran while one was open for 4% of the time, Pallas kernels for 0%

profile of v1, /device:TPU:1, one launch (start us, length us, event | category | flops | bytes accessed | tf_op | source)
XLA Modules:
  0.0 364.6 jit_solution(9623986976378854868)
XLA Ops:
  7.2 0.0 all-gather.3.cloned.1.call-start
  7.2 2.2 pad_maximum_fusion
  9.4 0.0 all-gather.3.cloned.1.call-update
  9.4 0.0 reduce-scatter.9.cloned.1.call-start
  9.5 1.0 reshape.28
  10.4 0.1 copy.31
  10.5 0.1 reshape.29
  10.6 10.7 %all_to_all.15 = bf16[4,16,1024]{2,1,0:T(8,128)(2,1)S(1)} all-to-all(bf16[4,16,1024]{2,1,0:T(8,128)(2,1)S(1)} %reshape.29), channel_id=1, replica_groups=mesh['xh'=2,'y'=4,'c'=2,'xl'=2,'z'=8] {'xh','c'}, dimensions={0} | all-to-all | bytes 262144 | tf_op jit(solution)/shard_map/all_to_all | solution.py:32
  21.3 0.2 stack.2
  21.6 54.8 %all_to_all.16 = bf16[16,4,16,1024]{3,2,1,0:T(8,128)(2,1)S(1)} all-to-all(bf16[16,4,16,1024]{3,2,1,0:T(8,128)(2,1)S(1)} %stack.2), channel_id=1, replica_groups=mesh['xh'=2,'y'=4,'c'=2,'xl'=2,'z'=8] {'xl','z'}, dimensions={0} | all-to-all | bytes 4194304 | tf_op jit(solution)/shard_map/all_to_all | solution.py:34
  76.3 0.2 copy.20
  76.5 0.0 all-gather.3.cloned.1.call-done
  76.5 7.7 %fusion = bf16[1024,1792]{0,1:T(8,128)(2,1)} fusion(bf16[1024,1792]{1,0:T(8,128)(2,1)} %all-gather.3.cloned.1.call-done, bf16[1024,1024]{1,0:T(8,128)(2,1)S(1)} %bitcast.40), kind=kOutput, calls=%fused_computation.2 | convolution fusion | flops 3759931392 | bytes 9437184 | tf_op jit(solution)/shard_map/dot_general | solution.py:40
  84.2 0.0 reduce-scatter.9.cloned.1.call-update
  84.3 0.0 all-gather.5.cloned.1.call-start
  84.3 0.9 copy-done
  85.2 0.2 copy.21
  85.5 52.2 %reduce-scatter.9.cloned.1.call-done = bf16[256,1792]{0,1:T(8,128)(2,1)} async-done(((bf16[1024,1792]{0,1:T(8,128)(2,1)}), bf16[256,1792]{0,1:T(8,128)(2,1)}) %reduce-scatter.9.cloned.1.call-update) | async-done | bytes 917520 | tf_op jit(solution)/shard_map/reduce_scatter | solution.py:41
  137.7 1.3 convert_element_type.32
  139.0 0.7 fusion.3
  139.7 1.0 pad_maximum_fusion.1
  140.7 0.0 all-gather.5.cloned.1.call-update
  140.8 0.0 all-reduce.5.cloned.1.call-start
  140.8 38.6 %all-gather.5.cloned.1.call-done = bf16[1024,1792]{0,1:T(8,128)(2,1)} async-done(((bf16[256,1792]{0,1:T(8,128)(2,1)}), bf16[1024,1792]{0,1:T(8,128)(2,1)}) %all-gather.5.cloned.1.call-update) | async-done | bytes 3670032 | tf_op jit(solution)/shard_map/all_gather | solution.py:43
  179.4 8.6 %convolution_convert_fusion.2 = bf16[1024,1024]{1,0:T(8,128)(2,1)} fusion(bf16[1024,1792]{0,1:T(8,128)(2,1)} %all-gather.5.cloned.1.call-done, bf16[1024,1792]{1,0:T(8,128)(2,1)} %all-gather.3.cloned.1.call-done), kind=kOutput, calls=%fused_computation.4 | convolution fusion | flops 3759144960 | bytes 9437184 | tf_op jit(solution)/shard_map/dot_general | solution.py:46
  187.9 0.0 all-reduce.5.cloned.1.call-update
  187.9 0.0 all-reduce.7.cloned.1.call-start
  188.0 0.6 dynamic-slice
  188.6 77.5 %all-reduce.5.cloned.1.call-done = bf16[8,2,4,16,1024]{4,3,0,1,2:T(8,128)(2,1)} async-done(((bf16[8,2,4,16,1024]{4,3,0,1,2:T(8,128)(2,1)}), bf16[8,2,4,16,1024]{4,3,0,1,2:T(8,128)(2,1)}) %all-reduce.5.cloned.1.call-update) | async-done | bytes 2097168
  266.1 2.3 dynamic-slice_bitcast_fusion
  268.4 0.0 all-reduce.7.cloned.1.call-update
  268.4 0.0 reduce-scatter.11.cloned.1.call-start
  268.5 7.6 %fusion.1 = bf16[1024,1792]{0,1:T(8,128)(2,1)} fusion(bf16[1024,1792]{0,1:T(8,128)(2,1)} %all-gather.5.cloned.1.call-done, bf16[1024,1024]{1,0:T(8,128)(2,1)S(1)} %bitcast.41), kind=kOutput, calls=%fused_computation.3 | convolution fusion | flops 3759931392 | bytes 9437184 | tf_op jit(solution)/shard_map/dot_general | solution.py:55
  276.0 0.0 reduce-scatter.11.cloned.1.call-update
  276.1 0.7 copy-done.1
  276.7 0.6 dynamic-slice.2
  277.3 28.2 %all-reduce.7.cloned.1.call-done = bf16[2,4,16,1024]{3,2,0,1:T(8,128)(2,1)} async-done(((bf16[2,4,16,1024]{3,2,0,1:T(8,128)(2,1)}), bf16[2,4,16,1024]{3,2,0,1:T(8,128)(2,1)}) %all-reduce.7.cloned.1.call-update) | async-done | bytes 262160
  305.5 2.2 dynamic-slice_bitcast_fusion.1
  307.8 5.1 %all-to-all-start.2 = ((bf16[4,16,1024]{2,1,0:T(8,128)(2,1)}), bf16[4,16,1024]{2,1,0:T(8,128)(2,1)S(1)}, u32[]{:S(2)}, u32[]{:S(2)}) async-start(bf16[4,16,1024]{2,1,0:T(8,128)(2,1)} %dynamic-slice_bitcast_fusion.1), calls=%async_computation.3 | async-start | bytes 262144 | tf_op jit(solution)/shard_map/all_to_all | solution.py:53
  312.8 1.0 copy.23
  313.8 4.1 %all-to-all-done.2 = bf16[4,16,1024]{2,1,0:T(8,128)(2,1)S(1)} async-done(((bf16[4,16,1024]{2,1,0:T(8,128)(2,1)}), bf16[4,16,1024]{2,1,0:T(8,128)(2,1)S(1)}, u32[]{:S(2)}, u32[]{:S(2)}) %all-to-all-start.2) | async-done | bytes 131104 | tf_op jit(solution)/shard_map/all_to_all | solution.py:53
  317.9 0.1 reshape.32
  318.0 0.1 copy.22
  318.2 0.7 reshape.33
  318.9 35.7 %reduce-scatter.11.cloned.1.call-done = bf16[256,1792]{0,1:T(8,128)(2,1)} async-done(((bf16[1024,1792]{0,1:T(8,128)(2,1)}), bf16[256,1792]{0,1:T(8,128)(2,1)}) %reduce-scatter.11.cloned.1.call-update) | async-done | bytes 917520 | tf_op jit(solution)/shard_map/reduce_scatter | solution.py:58
  354.6 1.2 fusion.6
  355.8 1.0 copy.24
  356.8 1.0 copy.25
  (4 shorter events, 0.0 us)
Async XLA Ops:
  7.2 69.3 %all-gather.3.cloned.1.call-start = ((), (), s32[]{:S(2)}) async-start(), calls=%async_computation.5 | async-start | bytes 4587520 | tf_op jit(solution)/shard_map/all_gather | solution.py:37
  9.4 128.3 %reduce-scatter.9.cloned.1.call-start = ((), (), s32[]{:S(2)}) async-start(), calls=%async_computation.6 | async-start | bytes 4587520 | tf_op jit(solution)/shard_map/reduce_scatter | solution.py:41
  84.2 1.0 copy-start
  84.3 95.1 %all-gather.5.cloned.1.call-start = ((), (), s32[]{:S(2)}) async-start(), calls=%async_computation.7 | async-start | bytes 4587520 | tf_op jit(solution)/shard_map/all_gather | solution.py:43
  140.7 47.3 %copy-start.2 = (u32[256]{0:T(256)S(1)}, u32[256]{0:T(256)}, u32[]{:S(2)}) copy-start(u32[256]{0:T(256)} %constant.5) | copy-start | bytes 3076
  140.8 125.3 %all-reduce.5.cloned.1.call-start = ((), (), s32[]{:S(2)}) async-start(), calls=%async_computation.9 | async-start | bytes 4194304
  187.9 117.6 %all-reduce.7.cloned.1.call-start = ((), (), s32[]{:S(2)}) async-start(), calls=%async_computation.10 | async-start | bytes 524288
  268.4 86.2 %reduce-scatter.11.cloned.1.call-start = ((), (), s32[]{:S(2)}) async-start(), calls=%async_computation.8 | async-start | bytes 4587520 | tf_op jit(solution)/shard_map/reduce_scatter | solution.py:58
  276.0 0.7 copy-start.1
  307.8 10.2 %all-to-all-start.2 = ((bf16[4,16,1024]{2,1,0:T(8,128)(2,1)}), bf16[4,16,1024]{2,1,0:T(8,128)(2,1)S(1)}, u32[]{:S(2)}, u32[]{:S(2)}) async-start(bf16[4,16,1024]{2,1,0:T(8,128)(2,1)} %dynamic-slice_bitcast_fusion.1), calls=%async_computation.3 | async-start | bytes 262144 | tf_op jit(solution)/shard_map/all_to_all | solution.py:53
Sparse Core Ops, SparseCore 0:
  9.8 50.2 all-gather.2
  84.4 53.2 reduce-scatter.8
  140.9 38.4 all-gather.4
  188.1 77.9 all-reduce.4
  269.3 36.2 all-reduce.6
  308.0 46.6 reduce-scatter.10
